TPU v7x, 32 devices: a whole 2x2x4 slice. The times are simulated.
32 devices in a mesh: rep: 2 (over x), dp: 4 (over y, core), ctx: 4 (over z).
Axes of the slice: x: 2, y: 2, z: 4, core: 2. Of those that a mesh axis runs over, the one named last changes fastest.
Arguments:
- frames: bfloat16 [8, 512, 1024], P(('rep', 'dp'), 'ctx'), may hold values from -24 to 24
- lengths: int32 [8], P(('rep', 'dp')), may hold values from 64 to 512, as said below
- cotangent: bfloat16 [8, 512, 1024], P(('rep', 'dp'), 'ctx'), may hold values from -6 to 6
- w_query: bfloat16 [1024, 512], P('dp'), may hold values from -0.5 to 0.5
- w_key: bfloat16 [1024, 512], P('dp'), may hold values from -0.5 to 0.5
- w_value: bfloat16 [1024, 512], P('dp'), may hold values from -0.1875 to 0.1875
- w_out: bfloat16 [512, 1024], P('dp'), may hold values from -0.25 to 0.25
Outputs:
- attended: bfloat16 [8, 512, 1024], P(('rep', 'dp'), 'ctx')
- grad_frames: bfloat16 [8, 512, 1024], P(('rep', 'dp'), 'ctx')
- grad_out: float32 [512, 1024], P('dp')
Inputs may be any that keep to these rules, and one draw needn't show every extreme that they name: `lengths`: number of real frames of each meeting; one meeting of every draw has all 512 frames real.
All inputs are finite; a program needn't handle non-finite values.
Results may differ from a plain program's by a relative error of at most 0.025.
The roundings to bfloat16 on the way count: a program that leaves them out, or rounds other values in their place, can miss the bound.
Values may be sent and summed in bfloat16 or wider, within the bound.
A program may use at most 64 MiB of HBM per device.

v0:
```python
import math

import jax
import jax.numpy as jnp
from jax import lax
from jax.sharding import PartitionSpec as P

HEAD = 128


MASKED_SCORE = -1e30


def head_split(matrix, head_count):
    return matrix.reshape(matrix.shape[0], head_count, matrix.shape[1] // head_count)


def forward_step(carry, key_part, value_part, offset, query_heads, length, score_scale):
    head_count = query_heads.shape[1]
    amount = key_part.shape[0]
    maxima, totals, accumulated = carry
    key_heads = head_split(key_part, head_count)
    value_heads = head_split(value_part, head_count)
    scores = (
        jnp.einsum("rhe,nhe->hrn", query_heads, key_heads, preferred_element_type=jnp.float32)
        * score_scale
    )
    usable = offset + jnp.arange(amount) < length
    scores = jnp.where(usable[None, None, :], scores, MASKED_SCORE)
    new_maxima = jnp.maximum(maxima, jnp.max(scores, axis=2))
    factor = jnp.exp(maxima - new_maxima)
    exponent = jnp.where(usable[None, None, :], jnp.exp(scores - new_maxima[:, :, None]), 0.0)
    totals = totals * factor + jnp.sum(exponent, axis=2)
    mixed = jnp.einsum(
        "hrn,nhe->hre",
        exponent.astype(jnp.bfloat16),
        value_heads,
        preferred_element_type=jnp.float32,
    )
    accumulated = accumulated * factor[:, :, None] + mixed
    return (new_maxima, totals, accumulated)


def query_step(
    grad_accum,
    key_part,
    value_part,
    offset,
    query_heads,
    context_heads,
    logsum,
    deltas,
    length,
    score_scale,
):
    head_count = query_heads.shape[1]
    amount = key_part.shape[0]
    key_heads = head_split(key_part, head_count)
    value_heads = head_split(value_part, head_count)
    scores = (
        jnp.einsum("rhe,nhe->hrn", query_heads, key_heads, preferred_element_type=jnp.float32)
        * score_scale
    )
    usable = offset + jnp.arange(amount) < length
    attention = jnp.where(usable[None, None, :], jnp.exp(scores - logsum[:, :, None]), 0.0)
    grad_prob = jnp.einsum(
        "rhe,nhe->hrn", context_heads, value_heads, preferred_element_type=jnp.float32
    )
    grad_score = (attention * (grad_prob - deltas[:, :, None])).astype(jnp.bfloat16)
    added = jnp.einsum("hrn,nhe->rhe", grad_score, key_heads, preferred_element_type=jnp.float32)
    return grad_accum + added * score_scale


def key_step(
    query_part,
    context_part,
    all_logsum,
    all_deltas,
    key_heads,
    value_heads,
    key_usable,
    score_scale,
):
    head_count = key_heads.shape[1]
    query_heads = head_split(query_part, head_count)
    context_heads = head_split(context_part, head_count)
    scores = (
        jnp.einsum("rhe,nhe->hrn", query_heads, key_heads, preferred_element_type=jnp.float32)
        * score_scale
    )
    attention = jnp.where(key_usable[None, None, :], jnp.exp(scores - all_logsum[:, :, None]), 0.0)
    grad_value = jnp.einsum(
        "hrn,rhe->nhe",
        attention.astype(jnp.bfloat16),
        context_heads,
        preferred_element_type=jnp.float32,
    )
    grad_prob = jnp.einsum(
        "rhe,nhe->hrn", context_heads, value_heads, preferred_element_type=jnp.float32
    )
    grad_score = (attention * (grad_prob - all_deltas[:, :, None])).astype(jnp.bfloat16)
    added = jnp.einsum("hrn,rhe->nhe", grad_score, query_heads, preferred_element_type=jnp.float32)
    return (added * score_scale, grad_value)


def back_project(gradient, weight):
    return lax.dot_general(
        gradient, weight, (((1,), (1,)), ((), ())), preferred_element_type=jnp.float32
    )


def shards(frames, lengths, cotangent, w_query, w_key, w_value, w_out):
    full_query, full_key, full_value, full_out = (
        lax.all_gather(w_query, "dp", axis=0, tiled=True),
        lax.all_gather(w_key, "dp", axis=0, tiled=True),
        lax.all_gather(w_value, "dp", axis=0, tiled=True),
        lax.all_gather(w_out, "dp", axis=0, tiled=True),
    )
    inputs = frames[0]
    upstream = cotangent[0]
    length = lengths[0]
    row_count = inputs.shape[0]
    inner_width = full_query.shape[1]
    head_count = inner_width // HEAD
    score_scale = HEAD ** (-0.5)
    first_frame = lax.axis_index("ctx") * row_count
    row_usable = first_frame + jnp.arange(row_count) < length
    queries = jnp.dot(inputs, full_query, preferred_element_type=jnp.float32).astype(jnp.bfloat16)
    keys = jnp.dot(inputs, full_key, preferred_element_type=jnp.float32).astype(jnp.bfloat16)
    values = jnp.dot(inputs, full_value, preferred_element_type=jnp.float32).astype(jnp.bfloat16)
    query_heads = head_split(queries, head_count)
    key_heads = head_split(keys, head_count)
    value_heads = head_split(values, head_count)
    start_state = (
        jnp.full((head_count, row_count), MASKED_SCORE, jnp.float32),
        jnp.zeros((head_count, row_count), jnp.float32),
        jnp.zeros((head_count, row_count, HEAD), jnp.float32),
    )
    all_keys, all_values = (
        lax.all_gather(keys, "ctx", axis=0, tiled=True),
        lax.all_gather(values, "ctx", axis=0, tiled=True),
    )
    key_block = row_count * math.gcd(max(1, 512 // row_count), lax.axis_size("ctx"))
    block_count = all_keys.shape[0] // key_block
    key_blocks = all_keys.reshape(block_count, key_block, inner_width)
    value_blocks = all_values.reshape(block_count, key_block, inner_width)
    block_starts = jnp.arange(block_count, dtype=jnp.int32) * key_block

    def scan_forward(current, scan_item):
        return (
            forward_step(
                current, scan_item[0], scan_item[1], scan_item[2], query_heads, length, score_scale
            ),
            None,
        )

    softmax_state, unused = lax.scan(
        scan_forward, start_state, (key_blocks, value_blocks, block_starts)
    )
    maxima, totals, accumulated = softmax_state
    context = (
        (accumulated / totals[:, :, None])
        .transpose(1, 0, 2)
        .reshape(row_count, inner_width)
        .astype(jnp.bfloat16)
    )
    logsum = maxima + jnp.log(totals)
    attended = jnp.dot(context, full_out, preferred_element_type=jnp.float32)
    attended = jnp.where(row_usable[:, None], attended, 0.0).astype(jnp.bfloat16)
    masked_grad = jnp.where(row_usable[:, None], upstream, jnp.zeros_like(upstream))
    grad_context = back_project(masked_grad, full_out).astype(jnp.bfloat16)
    deltas = jnp.sum(
        (grad_context.astype(jnp.float32) * context.astype(jnp.float32)).reshape(
            row_count, head_count, HEAD
        ),
        axis=2,
    )
    context_heads = head_split(grad_context, head_count)
    delta_heads = deltas.T
    all_logsum, all_deltas = (
        lax.all_gather(logsum, "ctx", axis=1, tiled=True),
        lax.all_gather(delta_heads, "ctx", axis=1, tiled=True),
    )
    zero_grad = jnp.zeros((row_count, head_count, HEAD), jnp.float32)

    def scan_query(current, scan_item):
        return (
            query_step(
                current,
                scan_item[0],
                scan_item[1],
                scan_item[2],
                query_heads,
                context_heads,
                logsum,
                delta_heads,
                length,
                score_scale,
            ),
            None,
        )

    grad_query, unused = lax.scan(scan_query, zero_grad, (key_blocks, value_blocks, block_starts))
    grad_key, grad_value = key_step(
        lax.all_gather(queries, "ctx", axis=0, tiled=True),
        lax.all_gather(grad_context, "ctx", axis=0, tiled=True),
        all_logsum,
        all_deltas,
        key_heads,
        value_heads,
        row_usable,
        score_scale,
    )
    grad_query = grad_query.reshape(row_count, inner_width).astype(jnp.bfloat16)
    grad_key = grad_key.reshape(row_count, inner_width).astype(jnp.bfloat16)
    grad_value = grad_value.reshape(row_count, inner_width).astype(jnp.bfloat16)
    grad_input = (
        back_project(grad_query, full_query)
        + back_project(grad_key, full_key)
        + back_project(grad_value, full_value)
    )
    grad_frames = grad_input.astype(jnp.bfloat16)
    summed_grad = lax.psum(
        lax.dot_general(
            context, masked_grad, (((0,), (0,)), ((), ())), preferred_element_type=jnp.float32
        ),
        ("rep", "ctx"),
    )
    grad_out = lax.psum_scatter(summed_grad, "dp", scatter_dimension=0, tiled=True)
    return (attended[None], grad_frames[None], grad_out)


def solution(mesh):
    in_specs = (
        P(("rep", "dp"), "ctx", None),
        P(("rep", "dp")),
        P(("rep", "dp"), "ctx", None),
        P("dp", None),
        P("dp", None),
        P("dp", None),
        P("dp", None),
    )
    out_specs = (P(("rep", "dp"), "ctx", None), P(("rep", "dp"), "ctx", None), P("dp", None))
    return jax.shard_map(shards, mesh=mesh, in_specs=in_specs, out_specs=out_specs, check_vma=False)
```

profile of v0, /device:TPU:13, one launch (start us, length us, event | category | flops | bytes accessed | tf_op | source)
XLA Modules:
  0.0 232.7 jit_solution(8206433220303085801)
XLA Ops:
  7.2 0.7 all-gather.9.cloned.1.call-update
  7.9 0.0 all-gather.7.cloned.1.call-start
  8.0 0.7 all-gather.7.cloned.1.call-update
  8.7 0.0 all-gather.5.cloned.1.call-start
  8.7 0.7 all-gather.5.cloned.1.call-update
  9.4 0.0 all-gather.11.cloned.1.call-start
  9.4 0.5 all-gather.11.cloned.1.call-update
  10.0 0.0 reduce-scatter.2.cloned.1.call-start
  10.7 16.2 %all-gather.9.cloned.1.call-done = bf16[1024,512]{1,0:T(8,128)(2,1)} async-done(((bf16[256,512]{1,0:T(8,128)(2,1)}), bf16[1024,512]{1,0:T(8,128)(2,1)}) %all-gather.9.cloned.1.call-update) | async-done | bytes 1048592 | tf_op jit(solution)/shard_map/all_gather | solution.py:116
  26.9 1.5 convolution_convert_fusion.2
  28.5 13.5 %all_gather.34 = bf16[512,512]{1,0:T(8,128)(2,1)S(1)} all-gather(bf16[128,512]{1,0:T(8,128)(2,1)S(1)} %convolution_convert_fusion.2), channel_id=1, replica_groups=mesh['rep'=2,'dp'=4,'ctx'=4] {'ctx'}, dimensions={0}, use_global_device_ids=true | all-gather | bytes 655360 | tf_op jit(solution)/shard_map/all_gather | solution.py:141
  41.9 0.2 copy.33
  42.2 3.1 %all-gather.7.cloned.1.call-done = bf16[1024,512]{1,0:T(8,128)(2,1)} async-done(((bf16[256,512]{1,0:T(8,128)(2,1)}), bf16[1024,512]{1,0:T(8,128)(2,1)}) %all-gather.7.cloned.1.call-update) | async-done | bytes 1048592 | tf_op jit(solution)/shard_map/all_gather | solution.py:115
  45.2 1.5 convolution_convert_fusion.3
  46.8 13.4 %all_gather.32 = bf16[512,512]{1,0:T(8,128)(2,1)S(1)} all-gather(bf16[128,512]{1,0:T(8,128)(2,1)S(1)} %convolution_convert_fusion.3), channel_id=1, replica_groups=mesh['rep'=2,'dp'=4,'ctx'=4] {'ctx'}, dimensions={0}, use_global_device_ids=true | all-gather | bytes 655360 | tf_op jit(solution)/shard_map/all_gather | solution.py:140
  60.2 0.2 copy.35
  60.4 3.2 %all-gather.5.cloned.1.call-done = bf16[1024,512]{1,0:T(8,128)(2,1)} async-done(((bf16[256,512]{1,0:T(8,128)(2,1)}), bf16[1024,512]{1,0:T(8,128)(2,1)}) %all-gather.5.cloned.1.call-update) | async-done | bytes 1048592 | tf_op jit(solution)/shard_map/all_gather | solution.py:114
  63.6 1.5 convolution_convert_fusion.4
  65.1 0.4 select_reduce_fusion
  65.5 0.3 fusion.23
  65.9 0.4 fusion.19
  66.3 0.2 copy-done.5
  66.5 1.8 fusion.36
  68.3 0.0 all-reduce.2.cloned.1.call-start
  68.4 0.1 copy.22
  68.5 0.8 copy.34
  69.2 12.5 %all-gather.11.cloned.1.call-done = bf16[512,1024]{1,0:T(8,128)(2,1)} async-done(((bf16[128,1024]{1,0:T(8,128)(2,1)}), bf16[512,1024]{1,0:T(8,128)(2,1)}) %all-gather.11.cloned.1.call-update) | async-done | bytes 1048592 | tf_op jit(solution)/shard_map/all_gather | solution.py:117
  81.7 1.7 convert_multiply_fusion
  83.5 0.1 reshape.104
  83.6 0.2 reduce_sum.23
  83.8 0.6 copy.23
  84.4 13.4 %all_gather.36 = bf16[512,512]{1,0:T(8,128)(2,1)S(1)} all-gather(bf16[128,512]{1,0:T(8,128)(2,1)S(1)} %convolution_convert_fusion.4), channel_id=1, replica_groups=mesh['rep'=2,'dp'=4,'ctx'=4] {'ctx'}, dimensions={0}, use_global_device_ids=true | all-gather | bytes 655360 | tf_op jit(solution)/shard_map/all_gather | solution.py:205
  97.8 1.1 copy.36
  98.8 13.6 %all_gather.38 = bf16[512,512]{1,0:T(8,128)(2,1)S(1)} all-gather(bf16[128,512]{1,0:T(8,128)(2,1)S(1)} %get-tuple-element.50), channel_id=1, replica_groups=mesh['rep'=2,'dp'=4,'ctx'=4] {'ctx'}, dimensions={0}, use_global_device_ids=true | all-gather | bytes 655360 | tf_op jit(solution)/shard_map/all_gather | solution.py:206
  112.4 0.2 copy.37
  112.7 11.5 %all_gather.39 = f32[4,512]{0,1:T(8,128)S(1)} all-gather(f32[4,128]{0,1:T(8,128)S(1)} %bitcast.109), channel_id=1, replica_groups=mesh['rep'=2,'dp'=4,'ctx'=4] {'ctx'}, dimensions={1}, use_global_device_ids=true | all-gather | bytes 10240 | tf_op jit(solution)/shard_map/all_gather | solution.py:182
  124.2 0.1 copy.27
  124.3 9.7 %all_gather.37 = f32[4,512]{1,0:T(4,128)S(1)} all-gather(f32[4,128]{1,0:T(4,128)S(1)} %get-tuple-element.36), channel_id=1, replica_groups=mesh['rep'=2,'dp'=4,'ctx'=4] {'ctx'}, dimensions={1}, use_global_device_ids=true | all-gather | bytes 10240 | tf_op jit(solution)/shard_map/all_gather | solution.py:181
  134.0 1.6 fusion.3
  135.6 1.0 convolution_convert_fusion
  136.6 2.3 fusion.18
  139.0 2.7 %fusion.60 = f32[128,1024]{1,0:T(8,128)} fusion(bf16[128,512]{0,1:T(8,128)(2,1)} %bitcast.115, bf16[1024,512]{1,0:T(8,128)(2,1)} %all-gather.5.cloned.1.call-done), kind=kOutput, calls=%fused_computation.80 | convolution fusion | flops 134217728 | bytes 1703936 | tf_op jit(solution)/shard_map/dot_general | solution.py:107
  141.6 2.9 %fusion.17 = bf16[4,128,128]{2,1,0:T(8,128)(2,1)} fusion(bf16[512,4,128]{0,2,1:T(8,128)(2,1)} %bitcast.104, f32[4,512,128]{2,1,0:T(8,128)} %copy-done.4, bf16[512,4,128]{0,2,1:T(8,128)(2,1)S(1)} %bitcast.100, bf16[128,4,128]{0,2,1:T(8,128)(2,1)} %bitcast.111, f32[4,512]{1,0:T(4,128)S(1)} %copy.27), kind=kOutput, calls=%fused_computation.30 | convolution fusion | flops 135135232 | bytes 2367488 | tf_op jit(solution)/shard_map/hrn,rhe->nhe/dot_general | solution.py:102
  144.6 1.0 fusion.14
  145.6 1.6 convolution_add_fusion.1
  147.2 1.2 fusion.13
  148.4 75.6 %all-reduce.2.cloned.1.call-done = f32[128,1024]{1,0:T(8,128)} async-done(((f32[128,1024]{1,0:T(8,128)}), f32[128,1024]{1,0:T(8,128)}) %all-reduce.2.cloned.1.call-update) | async-done | bytes 524304 | tf_op jit(solution)/shard_map/psum | solution.py:223
  224.0 1.9 copy.58
  (30 shorter events, 0.2 us)
Async XLA Ops:
  7.2 19.8 %copy-start = (bf16[1,128,1024]{2,1,0:T(8,128)(2,1)S(1)}, bf16[1,128,1024]{2,1,0:T(8,128)(2,1)}, u32[]{:S(2)}) copy-start(bf16[1,128,1024]{2,1,0:T(8,128)(2,1)} %param.7) | copy-start | bytes 786436
  7.2 19.7 %all-gather.9.cloned.1.call-start = ((), (), s32[]{:S(2)}) async-start(), calls=%async_computation.3 | async-start | bytes 1310720 | tf_op jit(solution)/shard_map/all_gather | solution.py:116
  7.9 37.3 %all-gather.7.cloned.1.call-start = ((), (), s32[]{:S(2)}) async-start(), calls=%async_computation.2 | async-start | bytes 1310720 | tf_op jit(solution)/shard_map/all_gather | solution.py:115
  8.7 54.9 %all-gather.5.cloned.1.call-start = ((), (), s32[]{:S(2)}) async-start(), calls=%async_computation.1 | async-start | bytes 1310720 | tf_op jit(solution)/shard_map/all_gather | solution.py:114
  9.4 72.3 %all-gather.11.cloned.1.call-start = ((), (), s32[]{:S(2)}) async-start(), calls=%async_computation.4 | async-start | bytes 1310720 | tf_op jit(solution)/shard_map/all_gather | solution.py:117
  10.0 134.5 %reduce-scatter.2.cloned.1.call-start = ((), (), s32[]{:S(2)}) async-start(), calls=%async_computation.5 | async-start | bytes 2621440 | tf_op jit(solution)/shard_map/reduce_scatter | solution.py:229
  10.7 55.2 %copy-start.10 = (pred[512]{0:T(512)(128)(4,1)}, pred[512]{0:T(512)(128)(4,1)S(1)}, u32[]{:S(2)}) copy-start(pred[512]{0:T(512)(128)(4,1)S(1)} %iota_compare_fusion) | copy-start | bytes 1540
  42.2 23.7 %copy-start.6 = (bf16[512,512]{0,1:T(8,128)(2,1)}, bf16[512,512]{0,1:T(8,128)(2,1)S(1)}, u32[]{:S(2)}) copy-start(bf16[512,512]{0,1:T(8,128)(2,1)S(1)} %copy.33) | copy-start | bytes 1572868
  46.8 18.3 %copy-start.7 = (bf16[128,512]{1,0:T(8,128)(2,1)}, bf16[128,512]{1,0:T(8,128)(2,1)S(1)}, u32[]{:S(2)}) copy-start(bf16[128,512]{1,0:T(8,128)(2,1)S(1)} %convolution_convert_fusion.3) | copy-start | bytes 393220
  65.5 1.0 copy-start.5
  68.3 155.6 %all-reduce.2.cloned.1.call-start = ((), (), s32[]{:S(2)}) async-start(), calls=%async_computation.6 | async-start | bytes 1048576 | tf_op jit(solution)/shard_map/psum | solution.py:223
  83.5 29.2 %copy-start.8 = (bf16[128,512]{1,0:T(8,128)(2,1)}, bf16[128,512]{1,0:T(8,128)(2,1)S(1)}, u32[]{:S(2)}) copy-start(bf16[128,512]{1,0:T(8,128)(2,1)S(1)} %get-tuple-element.50) | copy-start | bytes 393220
  135.6 3.4 %copy-start.4 = (f32[4,512,128]{2,1,0:T(8,128)}, f32[4,512,128]{2,1,0:T(8,128)S(1)}, u32[]{:S(2)}) copy-start(f32[4,512,128]{2,1,0:T(8,128)S(1)} %fusion.3) | copy-start | bytes 3145732
  139.0 5.6 %copy-start.2 = (bf16[512,1024]{1,0:T(8,128)(2,1)S(1)}, bf16[512,1024]{1,0:T(8,128)(2,1)}, u32[]{:S(2)}) copy-start(bf16[512,1024]{1,0:T(8,128)(2,1)} %all-gather.11.cloned.1.call-done) | copy-start | bytes 3145732
  141.6 4.0 %copy-start.1 = (bf16[1024,512]{1,0:T(8,128)(2,1)S(1)}, bf16[1024,512]{1,0:T(8,128)(2,1)}, u32[]{:S(2)}) copy-start(bf16[1024,512]{1,0:T(8,128)(2,1)} %all-gather.7.cloned.1.call-done) | copy-start | bytes 3145732
  144.5 2.7 %copy-start.3 = (bf16[1024,512]{1,0:T(8,128)(2,1)S(1)}, bf16[1024,512]{1,0:T(8,128)(2,1)}, u32[]{:S(2)}) copy-start(bf16[1024,512]{1,0:T(8,128)(2,1)} %all-gather.9.cloned.1.call-done) | copy-start | bytes 3145732
  144.5 2.7 %copy-start.9 = (bf16[4,128,128]{2,1,0:T(8,128)(2,1)S(1)}, bf16[4,128,128]{2,1,0:T(8,128)(2,1)}, u32[]{:S(2)}) copy-start(bf16[4,128,128]{2,1,0:T(8,128)(2,1)} %convolution_convert_fusion) | copy-start | bytes 393220
Sparse Core Ops, SparseCore 0:
  9.6 17.3 all-gather.8
  28.5 16.7 all-gather.6
  46.8 16.7 all-gather.4
  65.0 16.7 all-gather.10
  84.1 31.0 reduce-scatter.1
  144.7 79.2 all-reduce.1
where the time goes:
time: 237 us; the launch traced here: 233 us
  waiting for transfers between devices  113 us (48%)
  blocking collectives  75.1 us (32%)
  matrix products  23.2 us (10%)
  between operations  15 us (6%)
  local copies, waits for them, and re-layouts  5.47 us (2%)
    psum x1, waiting for transfers between devices, shards(): lax.psum(lax.dot_general(context, masked_grad, (((0,), (0,)), ((), ())),...  75.6 us
    all_gather x1, waiting for transfers between devices, shards(): lax.all_gather(w_value, 'dp', axis=0, tiled=True)  16.2 us
    all_gather x1, blocking collectives, shards(): lax.all_gather(grad_context, 'ctx', axis=0, tiled=True)  13.6 us
    all_gather x1, blocking collectives, shards(): lax.all_gather(values, 'ctx', axis=0, tiled=True)  13.5 us
    all_gather x1, blocking collectives, shards(): lax.all_gather(keys, 'ctx', axis=0, tiled=True)  13.4 us
    all_gather x1, blocking collectives, shards(): lax.all_gather(queries, 'ctx', axis=0, tiled=True)  13.4 us
    all_gather x1, waiting for transfers between devices, shards(): lax.all_gather(w_out, 'dp', axis=0, tiled=True)  12.5 us
    all_gather x1, blocking collectives, shards(): lax.all_gather(delta_heads, 'ctx', axis=1, tiled=True)  11.5 us
  transfers between devices with their start and end apart: 6, of which 5 were waited for; matrix products, arithmetic and copies ran while one was open for 12% of the time, Pallas kernels for 0%

commit v1 on v0

--- a/solution.py
+++ b/solution.py
@@ -1,8 +1,11 @@
+import functools
 import math
 
 import jax
 import jax.numpy as jnp
 from jax import lax
+from jax.experimental import pallas as pl
+from jax.experimental.pallas import tpu as pltpu
 from jax.sharding import PartitionSpec as P
 
 HEAD = 128
@@ -230,6 +233,376 @@
     return (attended[None], grad_frames[None], grad_out)
 
 
+MESH = pl.DeviceIdType.MESH
+
+
+def dot(left, right, left_dim, right_dim):
+    return lax.dot_general(
+        left, right, (((left_dim,), (right_dim,)), ((), ())), preferred_element_type=jnp.float32
+    )
+
+
+def fused_kernel(
+    frames_ref,
+    length_ref,
+    cot_ref,
+    wq_ref,
+    wk_ref,
+    wv_ref,
+    wo_ref,
+    attended_ref,
+    grad_frames_ref,
+    grad_out_ref,
+    xs,
+    cs,
+    wq,
+    wk,
+    wv,
+    wo,
+    qs,
+    ks,
+    vs,
+    gs,
+    ctx,
+    logsum,
+    deltas,
+    dq,
+    dk,
+    dv,
+    part,
+    part_in,
+    slices,
+    send_sem,
+    recv_sem,
+):
+    rep, dp, z = lax.axis_index("rep"), lax.axis_index("dp"), lax.axis_index("ctx")
+    count = 4
+    heads = 4
+    rows = frames_ref.shape[1]
+    full = rows * count
+    width = slices.shape[2]
+    scale = HEAD ** (-0.5)
+    sibling = dp + 1 - 2 * lax.rem(dp, 2)
+    across = lax.rem(dp + 2, 4)
+    across_sibling = lax.rem(sibling + 2, 4)
+    other_rep = 1 - rep
+    group = rep * 4 + dp
+
+    barrier = pltpu.get_barrier_semaphore()
+    for step in range(1, count):
+        pl.semaphore_signal(
+            barrier, inc=1, device_id=(rep, dp, lax.rem(z + step, count)), device_id_type=MESH
+        )
+    for step in range(1, 8):
+        peer = lax.rem(group + step, 8)
+        pl.semaphore_signal(
+            barrier, inc=1, device_id=(peer // 4, lax.rem(peer, 4), z), device_id_type=MESH
+        )
+    pl.semaphore_wait(barrier, 10)
+
+    def remote(source, target, index, device):
+        return pltpu.make_async_remote_copy(
+            src_ref=source,
+            dst_ref=target,
+            send_sem=send_sem.at[index],
+            recv_sem=recv_sem.at[index],
+            device_id=device,
+            device_id_type=MESH,
+        )
+
+    def chain(which, side, hop):
+        sign = 1 - 2 * side
+        home, pool = ((frames_ref, xs), (cot_ref, cs))[which]
+        owner = z - sign * (hop - 1)
+        source = home.at[0] if hop == 1 else pool.at[jnp.clip(owner, 0, count - 1)]
+        slot = jnp.clip(owner, 0, count - 1)
+        target = jnp.clip(z + sign, 0, count - 1)
+        index = which * 6 + side * 3 + hop - 1
+        valid = (z + sign >= 0) & (z + sign < count) & (owner >= 0) & (owner < count)
+        return valid, remote(source, pool.at[slot], index, (rep, dp, target))
+
+    def chain_send(which, hop):
+        for side in range(2):
+            valid, copy = chain(which, side, hop)
+
+            @pl.when(valid)
+            def _():
+                copy.start()
+
+    def chain_recv(which, hop):
+        for side in range(2):
+            sign = 1 - 2 * side
+            pool = (xs, cs)[which]
+            owner = z - sign * hop
+            slot = jnp.clip(owner, 0, count - 1)
+            index = which * 6 + side * 3 + hop - 1
+
+            @pl.when((owner >= 0) & (owner < count))
+            def _():
+                remote(pool.at[slot], pool.at[slot], index, (rep, dp, z)).wait_recv()
+
+    weights = ((wk_ref, wk), (wv_ref, wv), (wq_ref, wq), (wo_ref, wo))
+
+    def half(ref, which):
+        size = ref.shape[0] // 2
+        return ref.at[pl.ds(pl.multiple_of(which * size, size), size)]
+
+    def weight_copy(piece, step):
+        shard, pool = weights[piece]
+        index = 12 + piece * 5 + step
+        if step == 0:
+            return remote(shard, pool.at[dp], index, (rep, sibling, z))
+        if step == 1:
+            return remote(half(shard, rep), half(pool.at[dp], rep), index, (rep, across, z))
+        mine = pool.at[across]
+        if step == 2:
+            return remote(half(mine, rep), half(mine, rep), index, (rep, sibling, z))
+        if step == 3:
+            return remote(half(mine, rep), half(mine, rep), index, (other_rep, dp, z))
+        return remote(half(mine, other_rep), half(mine, other_rep), index, (rep, sibling, z))
+
+    def weight_recv(piece, step):
+        pool = weights[piece][1]
+        index = 12 + piece * 5 + step
+        if step == 0:
+            target = pool.at[sibling]
+        elif step == 1:
+            target = half(pool.at[across], rep)
+        elif step == 2:
+            target = half(pool.at[across_sibling], rep)
+        elif step == 3:
+            target = half(pool.at[across], other_rep)
+        else:
+            target = half(pool.at[across_sibling], other_rep)
+        remote(target, target, index, (rep, dp, z)).wait_recv()
+
+    chain_send(0, 1)
+    for piece in range(4):
+        weight_copy(piece, 1).start()
+    for piece in range(4):
+        weight_copy(piece, 0).start()
+    for shard, pool in weights:
+        pool[dp] = shard[...]
+    xs[z] = frames_ref[0]
+    cs[z] = cot_ref[0]
+
+    def pass_weights(piece):
+        weight_recv(piece, 1)
+        weight_copy(piece, 3).start()
+        weight_copy(piece, 2).start()
+
+    def finish_weights(piece):
+        weight_recv(piece, 3)
+        weight_copy(piece, 4).start()
+
+    pass_weights(0)
+    chain_recv(0, 1)
+    chain_send(0, 2)
+    chain_send(1, 1)
+    pass_weights(1)
+    finish_weights(0)
+    pass_weights(2)
+    finish_weights(1)
+    chain_recv(0, 2)
+    chain_send(0, 3)
+    pass_weights(3)
+    finish_weights(2)
+    finish_weights(3)
+    for piece in range(4):
+        for step in (0, 2, 4):
+            weight_recv(piece, step)
+    chain_recv(1, 1)
+    chain_send(1, 2)
+    chain_recv(0, 3)
+
+    length = length_ref[0]
+
+    def project(block, carry):
+        inputs = xs[block]
+        start = pl.multiple_of(block * rows, rows)
+        for pool, kept in ((wk, ks), (wv, vs), (wq, qs)):
+            matrix = dot(inputs, pool[...].reshape(1024, 512), 1, 0).astype(jnp.bfloat16)
+            for head in range(heads):
+                kept[head, pl.ds(start, rows), :] = matrix[:, head * HEAD : (head + 1) * HEAD]
+        return carry
+
+    lax.fori_loop(0, count, project, 0)
+
+    def key_mask(amount):
+        return lax.broadcasted_iota(jnp.int32, (amount, full), 1) < length
+
+    def forward(step, carry):
+        head = step // 2
+        amount = full // 2
+        start = pl.multiple_of(lax.rem(step, 2) * amount, amount)
+        usable = key_mask(amount)
+        scores = dot(qs[head, pl.ds(start, amount), :], ks[head], 1, 1) * scale
+        scores = jnp.where(usable, scores, MASKED_SCORE)
+        maxima = jnp.max(scores, axis=1, keepdims=True)
+        exponent = jnp.where(usable, jnp.exp(scores - maxima), 0.0)
+        totals = jnp.sum(exponent, axis=1, keepdims=True)
+        mixed = dot(exponent.astype(jnp.bfloat16), vs[head], 1, 0)
+        ctx[head, pl.ds(start, amount), :] = (mixed / totals).astype(jnp.bfloat16)
+        logsum[head, pl.ds(start, amount), :] = maxima + jnp.log(totals)
+        return carry
+
+    lax.fori_loop(0, 4, forward, 0)
+    chain_recv(1, 2)
+    chain_send(1, 3)
+    lax.fori_loop(4, 8, forward, 0)
+
+    own = pl.ds(pl.multiple_of(z * rows, rows), rows)
+    own_context = jnp.concatenate([ctx[head, own, :] for head in range(heads)], axis=1)
+    attended = dot(own_context, wo[...].reshape(512, 1024), 1, 0)
+    row_at = z * rows + lax.broadcasted_iota(jnp.int32, attended.shape, 0)
+    attended_ref[0] = jnp.where(row_at < length, attended, 0.0).astype(jnp.bfloat16)
+
+    chain_recv(1, 3)
+    for which in range(2):
+        for hop in range(1, count):
+            for side in range(2):
+                valid, copy = chain(which, side, hop)
+
+                @pl.when(valid)
+                def _():
+                    copy.wait_send()
+
+    def context_gradient(block, carry):
+        start = pl.multiple_of(block * rows, rows)
+        upstream = cs[block].astype(jnp.float32)
+        at = start + lax.broadcasted_iota(jnp.int32, upstream.shape, 0)
+        masked = jnp.where(at < length, upstream, 0.0).astype(jnp.bfloat16)
+        cs[block] = masked
+        matrix = dot(masked, wo[...].reshape(512, 1024), 1, 1).astype(jnp.bfloat16)
+        for head in range(heads):
+            piece = matrix[:, head * HEAD : (head + 1) * HEAD]
+            gs[head, pl.ds(start, rows), :] = piece
+            terms = piece.astype(jnp.float32) * ctx[head, pl.ds(start, rows), :].astype(jnp.float32)
+            deltas[head, pl.ds(start, rows), :] = jnp.sum(terms, axis=1, keepdims=True)
+        return carry
+
+    lax.fori_loop(0, count, context_gradient, 0)
+
+    columns = pl.ds(pl.multiple_of(z * width, width), width)
+    masked_slice = cs[:, :, columns].reshape(full, width)
+    for head in range(heads):
+        part[head] = dot(ctx[head], masked_slice, 0, 0).astype(jnp.bfloat16)
+
+    def part_copy(step):
+        peer = lax.rem(group + step, 8)
+        peer_dp = lax.rem(peer, 4)
+        return remote(part.at[peer_dp], part_in.at[step], 32 + step, (peer // 4, peer_dp, z))
+
+    for step in range(1, 8):
+        part_copy(step).start()
+
+    def backward(head, carry):
+        queries, keys, values, grads = qs[head], ks[head], vs[head], gs[head]
+        own_keys, own_values = ks[head, own, :], vs[head, own, :]
+        scores = dot(queries, own_keys, 1, 1) * scale
+        at = z * rows + lax.broadcasted_iota(jnp.int32, scores.shape, 1)
+        attention = jnp.where(at < length, jnp.exp(scores - logsum[head]), 0.0)
+        dv[head] = dot(attention.astype(jnp.bfloat16), grads, 0, 0).astype(jnp.bfloat16)
+        grad_prob = dot(grads, own_values, 1, 1)
+        grad_score = (attention * (grad_prob - deltas[head])).astype(jnp.bfloat16)
+        dk[head] = (dot(grad_score, queries, 0, 0) * scale).astype(jnp.bfloat16)
+        scores = dot(qs[head, own, :], keys, 1, 1) * scale
+        attention = jnp.where(key_mask(rows), jnp.exp(scores - logsum[head, own, :]), 0.0)
+        grad_prob = dot(gs[head, own, :], values, 1, 1)
+        grad_score = (attention * (grad_prob - deltas[head, own, :])).astype(jnp.bfloat16)
+        dq[head] = (dot(grad_score, keys, 1, 0) * scale).astype(jnp.bfloat16)
+        return carry
+
+    lax.fori_loop(0, heads, backward, 0)
+
+    total = part[dp].astype(jnp.float32)
+    for step in range(1, 8):
+        part_copy(step).wait_recv()
+        total = total + part_in[step].astype(jnp.float32)
+    slices[z] = total.astype(jnp.bfloat16)
+
+    def slice_copy(step):
+        return remote(
+            slices.at[z], slices.at[z], 40 + step, (rep, dp, lax.rem(z + step, count))
+        )
+
+    for step in range(1, count):
+        slice_copy(step).start()
+
+    grads = [
+        jnp.concatenate([kept[head] for head in range(heads)], axis=1) for kept in (dq, dk, dv)
+    ]
+    for shard in range(4):
+        added = (
+            dot(grads[0], wq[shard], 1, 1)
+            + dot(grads[1], wk[shard], 1, 1)
+            + dot(grads[2], wv[shard], 1, 1)
+        )
+        grad_frames_ref[0, :, shard * 256 : (shard + 1) * 256] = added.astype(jnp.bfloat16)
+
+    for piece in range(4):
+        for step in range(5):
+            weight_copy(piece, step).wait_send()
+    for step in range(1, 8):
+        part_copy(step).wait_send()
+    for step in range(1, count):
+        source = lax.rem(z + count - step, count)
+        remote(slices.at[source], slices.at[source], 40 + step, (rep, dp, z)).wait_recv()
+    for step in range(1, count):
+        slice_copy(step).wait_send()
+    for at in range(count):
+        grad_out_ref[:, at * width : (at + 1) * width] = slices[at].astype(jnp.float32)
+
+
+def fused(frames, lengths, cotangent, w_query, w_key, w_value, w_out):
+    vmem = pl.BlockSpec(memory_space=pltpu.VMEM)
+    bf16, f32 = jnp.bfloat16, jnp.float32
+    per_head = pltpu.VMEM((4, 512, HEAD), bf16)
+    own_head = pltpu.VMEM((4, 128, HEAD), bf16)
+    return pl.pallas_call(
+        fused_kernel,
+        out_shape=(
+            jax.ShapeDtypeStruct(frames.shape, bf16),
+            jax.ShapeDtypeStruct(frames.shape, bf16),
+            jax.ShapeDtypeStruct(w_out.shape, f32),
+        ),
+        in_specs=[vmem, pl.BlockSpec(memory_space=pltpu.SMEM)] + [vmem] * 5,
+        out_specs=(vmem, vmem, vmem),
+        scratch_shapes=[
+            pltpu.VMEM((4, 128, 1024), bf16),
+            pltpu.VMEM((4, 128, 1024), bf16),
+            pltpu.VMEM((4, 256, 512), bf16),
+            pltpu.VMEM((4, 256, 512), bf16),
+            pltpu.VMEM((4, 256, 512), bf16),
+            pltpu.VMEM((4, 128, 1024), bf16),
+            per_head,
+            per_head,
+            per_head,
+            per_head,
+            per_head,
+            pltpu.VMEM((4, 512, 1), f32),
+            pltpu.VMEM((4, 512, 1), f32),
+            own_head,
+            own_head,
+            own_head,
+            pltpu.VMEM((4, 128, 256), bf16),
+            pltpu.VMEM((8, 128, 256), bf16),
+            pltpu.VMEM((4, 128, 256), bf16),
+            pltpu.SemaphoreType.DMA((44,)),
+            pltpu.SemaphoreType.DMA((44,)),
+        ],
+        compiler_params=pltpu.CompilerParams(
+            collective_id=0, has_side_effects=True, vmem_limit_bytes=48 * 1024 * 1024
+        ),
+    )(frames, lengths, cotangent, w_query, w_key, w_value, w_out)
+
+
+def either(sizes, frames, lengths, cotangent, w_query, w_key, w_value, w_out):
+    fits = sizes == (2, 4, 4) and frames.shape == (1, 128, 1024) and w_query.shape == (256, 512)
+    chosen = fused if fits else shards
+    return chosen(frames, lengths, cotangent, w_query, w_key, w_value, w_out)
+
+
 def solution(mesh):
     in_specs = (
         P(("rep", "dp"), "ctx", None),
@@ -241,4 +614,6 @@
         P("dp", None),
     )
     out_specs = (P(("rep", "dp"), "ctx", None), P(("rep", "dp"), "ctx", None), P("dp", None))
-    return jax.shard_map(shards, mesh=mesh, in_specs=in_specs, out_specs=out_specs, check_vma=False)
+    sizes = (mesh.shape["rep"], mesh.shape["dp"], mesh.shape["ctx"])
+    body = functools.partial(either, sizes)
+    return jax.shard_map(body, mesh=mesh, in_specs=in_specs, out_specs=out_specs, check_vma=False)

time: 237 us -> 65.9 us (0.28); the launches traced: 233 us -> 65.6 us
  waiting for transfers between devices: 113 us -> 0 us
  blocking collectives: 75.1 us -> 0 us
  Pallas kernels: 0 us -> 56.4 us
  matrix products: 23.2 us -> 0 us
  between operations: 15 us -> 1.3 us
  local copies, waits for them, and re-layouts: 5.47 us -> 7.89 us
    psum x1 -> x0, waiting for transfers between devices: 75.6 us -> none  [shards(): lax.psum(lax.dot_general(context, masked_grad, (((0,), (0,)), ((), ())),...]
    all_gather x6 -> x0, blocking collectives: 75.1 us -> none  [the longest x1 13.6 us: shards(): lax.all_gather(grad_context, 'ctx', axis=0, tiled=True)]
    pallas_call x0 -> x1, Pallas kernels: none -> 56.4 us  [fused(): pl.pallas_call(fused_kernel, out_shape=(jax.ShapeDtypeStruct(frames.shape...]
    all_gather x4 -> x0, waiting for transfers between devices: 34.9 us -> none  [the longest x1 16.2 us: shards(): lax.all_gather(w_value, 'dp', axis=0, tiled=True)]
    dot_general x15 -> x0, matrix products: 23.2 us -> none  [the longest x4 7.14 us: back_project(): lax.dot_general(gradient, weight, (((1,), (1,)), ((), ())), preferred_ele...]
    unnamed x23 -> x15, local copies, waits for them, and re-layouts: 2.09 us -> 7.89 us
    unnamed x6 -> x0, waiting for transfers between devices: 2.61 us -> none
    reshape x6 -> x0, local copies, waits for them, and re-layouts: 2.54 us -> none  [the longest x5 2.45 us: head_split(): matrix.reshape(matrix.shape[0], head_count, matrix.shape[1] // head_count)]
  transfers between devices with their start and end apart: 6 -> 0, of which waited for: 5 -> 0; matrix products, arithmetic and copies ran while one was open for 12% -> 0% of each run, Pallas kernels for 0% -> 0%
where the time goes in v1:
time: 65.9 us; the launch traced here: 65.6 us
  Pallas kernels  56.4 us (86%)
  local copies, waits for them, and re-layouts  7.89 us (12%)
  between operations  1.3 us (2%)
    pallas_call x1, Pallas kernels, fused(): pl.pallas_call(fused_kernel, out_shape=(jax.ShapeDtypeStruct(frames.shape...  56.4 us
    unnamed x15, local copies, waits for them, and re-layouts  7.89 us

profile of v1, /device:TPU:13, one launch (start us, length us, event | category | flops | bytes accessed | tf_op | source)
XLA Modules:
  0.0 65.6 jit_solution(11232950149628312292)
XLA Ops:
  1.3 0.0 copy-start
  1.3 0.9 %copy-done = bf16[1,128,1024]{2,1,0:T(8,128)(2,1)S(1)} copy-done((bf16[1,128,1024]{2,1,0:T(8,128)(2,1)S(1)}, bf16[1,128,1024]{2,1,0:T(8,128)(2,1)}, u32[]{:S(2)}) %copy-start) | copy-done | bytes 262168
  2.2 0.0 copy-start.1
  2.2 0.9 %copy-done.1 = bf16[1,128,1024]{2,1,0:T(8,128)(2,1)S(1)} copy-done((bf16[1,128,1024]{2,1,0:T(8,128)(2,1)S(1)}, bf16[1,128,1024]{2,1,0:T(8,128)(2,1)}, u32[]{:S(2)}) %copy-start.1) | copy-done | bytes 262168
  3.2 0.0 copy-start.2
  3.2 0.9 %copy-done.2 = bf16[256,512]{1,0:T(8,128)(2,1)S(1)} copy-done((bf16[256,512]{1,0:T(8,128)(2,1)S(1)}, bf16[256,512]{1,0:T(8,128)(2,1)}, u32[]{:S(2)}) %copy-start.2) | copy-done | bytes 262168
  4.1 0.0 copy-start.3
  4.1 0.9 %copy-done.3 = bf16[256,512]{1,0:T(8,128)(2,1)S(1)} copy-done((bf16[256,512]{1,0:T(8,128)(2,1)S(1)}, bf16[256,512]{1,0:T(8,128)(2,1)}, u32[]{:S(2)}) %copy-start.3) | copy-done | bytes 262168
  5.1 0.0 copy-start.4
  5.1 0.9 %copy-done.4 = bf16[256,512]{1,0:T(8,128)(2,1)S(1)} copy-done((bf16[256,512]{1,0:T(8,128)(2,1)S(1)}, bf16[256,512]{1,0:T(8,128)(2,1)}, u32[]{:S(2)}) %copy-start.4) | copy-done | bytes 262168
  6.0 0.0 copy-start.5
  6.0 0.9 %copy-done.5 = bf16[128,1024]{1,0:T(8,128)(2,1)S(1)} copy-done((bf16[128,1024]{1,0:T(8,128)(2,1)S(1)}, bf16[128,1024]{1,0:T(8,128)(2,1)}, u32[]{:S(2)}) %copy-start.5) | copy-done | bytes 262168
  7.0 56.4 %shard_map.94 = (bf16[1,128,1024]{2,1,0:T(8,128)(2,1)S(1)}, bf16[1,128,1024]{2,1,0:T(8,128)(2,1)S(1)}, f32[128,1024]{1,0:T(8,128)S(1)}) custom-call(bf16[1,128,1024]{2,1,0:T(8,128)(2,1)S(1)} %copy-done, s32[1]{0:T(128)S(6)} %copy.13.length_ref, bf16[1,128,1024]{2,1,0:T(8,128)(2,1)S(1)} %copy-done.1, bf16[256,512]{1,0:T(8,128)(2,1)S(1)} %copy-done.2, ...), custom_call_target="tpu_custom_call" | custom-call | tf_op jit(solution)/shard_map/pallas_call | solution.py:562
  63.4 0.7 %copy.14 = bf16[1,128,1024]{2,1,0:T(8,128)(2,1)} copy(bf16[1,128,1024]{2,1,0:T(8,128)(2,1)S(1)} %get-tuple-element.6) | data formatting | bytes 524288
  64.1 0.7 %copy.15 = bf16[1,128,1024]{2,1,0:T(8,128)(2,1)} copy(bf16[1,128,1024]{2,1,0:T(8,128)(2,1)S(1)} %get-tuple-element.7) | data formatting | bytes 524288
  64.8 0.8 %copy.16 = f32[128,1024]{1,0:T(8,128)} copy(f32[128,1024]{1,0:T(8,128)S(1)} %get-tuple-element.8) | data formatting | bytes 1048576
Async XLA Ops:
  1.3 1.0 %copy-start = (bf16[1,128,1024]{2,1,0:T(8,128)(2,1)S(1)}, bf16[1,128,1024]{2,1,0:T(8,128)(2,1)}, u32[]{:S(2)}) copy-start(bf16[1,128,1024]{2,1,0:T(8,128)(2,1)} %frames_ref.1) | copy-start | bytes 786436
  2.2 0.9 %copy-start.1 = (bf16[1,128,1024]{2,1,0:T(8,128)(2,1)S(1)}, bf16[1,128,1024]{2,1,0:T(8,128)(2,1)}, u32[]{:S(2)}) copy-start(bf16[1,128,1024]{2,1,0:T(8,128)(2,1)} %cot_ref.1) | copy-start | bytes 786436
  3.2 0.9 %copy-start.2 = (bf16[256,512]{1,0:T(8,128)(2,1)S(1)}, bf16[256,512]{1,0:T(8,128)(2,1)}, u32[]{:S(2)}) copy-start(bf16[256,512]{1,0:T(8,128)(2,1)} %wq_ref.1) | copy-start | bytes 786436
  4.1 0.9 %copy-start.3 = (bf16[256,512]{1,0:T(8,128)(2,1)S(1)}, bf16[256,512]{1,0:T(8,128)(2,1)}, u32[]{:S(2)}) copy-start(bf16[256,512]{1,0:T(8,128)(2,1)} %wk_ref.1) | copy-start | bytes 786436
  5.1 0.9 %copy-start.4 = (bf16[256,512]{1,0:T(8,128)(2,1)S(1)}, bf16[256,512]{1,0:T(8,128)(2,1)}, u32[]{:S(2)}) copy-start(bf16[256,512]{1,0:T(8,128)(2,1)} %wv_ref.1) | copy-start | bytes 786436
  6.0 0.9 %copy-start.5 = (bf16[128,1024]{1,0:T(8,128)(2,1)S(1)}, bf16[128,1024]{1,0:T(8,128)(2,1)}, u32[]{:S(2)}) copy-start(bf16[128,1024]{1,0:T(8,128)(2,1)} %wo_ref.1) | copy-start | bytes 786436

commit v2 on v1

--- a/solution.py
+++ b/solution.py
@@ -254,6 +254,8 @@
     grad_frames_ref,
     grad_out_ref,
     xs,
+    upstream,
+    mine,
     cs,
     wq,
     wk,
@@ -274,6 +276,7 @@
     slices,
     send_sem,
     recv_sem,
+    local_sem,
 ):
     rep, dp, z = lax.axis_index("rep"), lax.axis_index("dp"), lax.axis_index("ctx")
     count = 4
@@ -288,6 +291,22 @@
     other_rep = 1 - rep
     group = rep * 4 + dp
 
+    local = [
+        pltpu.make_async_copy(source, target, local_sem.at[at])
+        for at, (source, target) in enumerate(
+            (
+                (wk_ref, wk.at[dp]),
+                (wv_ref, wv.at[dp]),
+                (wq_ref, wq.at[dp]),
+                (wo_ref, wo.at[dp]),
+                (frames_ref.at[0], xs.at[z]),
+                (cot_ref.at[0], upstream),
+            )
+        )
+    ]
+    for copy in local:
+        copy.start()
+
     barrier = pltpu.get_barrier_semaphore()
     for step in range(1, count):
         pl.semaphore_signal(
@@ -312,10 +331,10 @@
 
     def chain(which, side, hop):
         sign = 1 - 2 * side
-        home, pool = ((frames_ref, xs), (cot_ref, cs))[which]
+        pool = (xs, gs)[which]
         owner = z - sign * (hop - 1)
-        source = home.at[0] if hop == 1 else pool.at[jnp.clip(owner, 0, count - 1)]
         slot = jnp.clip(owner, 0, count - 1)
+        source = frames_ref.at[0] if which == 0 and hop == 1 else pool.at[slot]
         target = jnp.clip(z + sign, 0, count - 1)
         index = which * 6 + side * 3 + hop - 1
         valid = (z + sign >= 0) & (z + sign < count) & (owner >= 0) & (owner < count)
@@ -332,7 +351,7 @@
     def chain_recv(which, hop):
         for side in range(2):
             sign = 1 - 2 * side
-            pool = (xs, cs)[which]
+            pool = (xs, gs)[which]
             owner = z - sign * hop
             slot = jnp.clip(owner, 0, count - 1)
             index = which * 6 + side * 3 + hop - 1
@@ -341,92 +360,130 @@
             def _():
                 remote(pool.at[slot], pool.at[slot], index, (rep, dp, z)).wait_recv()
 
-    weights = ((wk_ref, wk), (wv_ref, wv), (wq_ref, wq), (wo_ref, wo))
+    weights = ((wo_ref, wo), (wk_ref, wk), (wv_ref, wv), (wq_ref, wq))
 
     def half(ref, which):
         size = ref.shape[0] // 2
         return ref.at[pl.ds(pl.multiple_of(which * size, size), size)]
 
+    def chunk(ref, which, at):
+        size = ref.shape[0] // 4
+        return ref.at[pl.ds(pl.multiple_of((which * 2 + at) * size, size), size)]
+
     def weight_copy(piece, step):
         shard, pool = weights[piece]
-        index = 12 + piece * 5 + step
+        index = 12 + piece * 7 + step
         if step == 0:
             return remote(shard, pool.at[dp], index, (rep, sibling, z))
-        if step == 1:
-            return remote(half(shard, rep), half(pool.at[dp], rep), index, (rep, across, z))
-        mine = pool.at[across]
-        if step == 2:
-            return remote(half(mine, rep), half(mine, rep), index, (rep, sibling, z))
-        if step == 3:
-            return remote(half(mine, rep), half(mine, rep), index, (other_rep, dp, z))
-        return remote(half(mine, other_rep), half(mine, other_rep), index, (rep, sibling, z))
+        if step < 3:
+            target = chunk(pool.at[dp], rep, step - 1)
+            return remote(chunk(shard, rep, step - 1), target, index, (rep, across, z))
+        mine_at = pool.at[across]
+        if step < 5:
+            source = chunk(mine_at, rep, step - 3)
+            return remote(source, source, index, (other_rep, dp, z))
+        source = half(mine_at, rep if step == 5 else other_rep)
+        return remote(source, source, index, (rep, sibling, z))
 
     def weight_recv(piece, step):
         pool = weights[piece][1]
-        index = 12 + piece * 5 + step
+        index = 12 + piece * 7 + step
         if step == 0:
             target = pool.at[sibling]
-        elif step == 1:
-            target = half(pool.at[across], rep)
-        elif step == 2:
-            target = half(pool.at[across_sibling], rep)
-        elif step == 3:
-            target = half(pool.at[across], other_rep)
+        elif step < 3:
+            target = chunk(pool.at[across], rep, step - 1)
+        elif step < 5:
+            target = chunk(pool.at[across], other_rep, step - 3)
         else:
-            target = half(pool.at[across_sibling], other_rep)
+            target = half(pool.at[across_sibling], rep if step == 5 else other_rep)
         remote(target, target, index, (rep, dp, z)).wait_recv()
 
+    def finish_chunk(at):
+        weight_recv(at // 2, 3 + at % 2)
+        if at % 2 == 1:
+            weight_copy(at // 2, 6).start()
+
+    def weight_chunk(at):
+        weight_recv(at // 2, 1 + at % 2)
+        weight_copy(at // 2, 3 + at % 2).start()
+        if at + 2 < 8:
+            weight_copy((at + 2) // 2, 1 + at % 2).start()
+        if at % 2 == 1:
+            weight_copy(at // 2, 5).start()
+        if at >= 2:
+            finish_chunk(at - 2)
+
+    def cot_copy(step):
+        peer = lax.rem(z + step, count)
+        return remote(mine.at[peer], cs.at[z], 52 + step, (rep, dp, peer))
+
     chain_send(0, 1)
-    for piece in range(4):
-        weight_copy(piece, 1).start()
+    for at in range(2):
+        weight_copy(0, 1 + at).start()
     for piece in range(4):
         weight_copy(piece, 0).start()
-    for shard, pool in weights:
-        pool[dp] = shard[...]
-    xs[z] = frames_ref[0]
-    cs[z] = cot_ref[0]
-
-    def pass_weights(piece):
-        weight_recv(piece, 1)
-        weight_copy(piece, 3).start()
-        weight_copy(piece, 2).start()
-
-    def finish_weights(piece):
-        weight_recv(piece, 3)
-        weight_copy(piece, 4).start()
-
-    pass_weights(0)
+    for copy in local:
+        copy.wait()
+
+    length = length_ref[0]
+    columns = [slice(at * width, (at + 1) * width) for at in range(count)]
+    real = z * rows + lax.broadcasted_iota(jnp.int32, (rows, width), 0) < length
+    for at in range(count):
+        kept = jnp.where(real, upstream[:, columns[at]].astype(jnp.float32), 0.0)
+        mine[at] = kept.astype(jnp.bfloat16)
+    cs[z] = mine[z]
+
+    for at in range(4):
+        weight_chunk(at)
     chain_recv(0, 1)
     chain_send(0, 2)
-    chain_send(1, 1)
-    pass_weights(1)
-    finish_weights(0)
-    pass_weights(2)
-    finish_weights(1)
+    for at in range(4, 6):
+        weight_chunk(at)
+    for step in (0, 5, 6):
+        weight_recv(0, step)
+    masked = jnp.concatenate([mine[at] for at in range(count)], axis=1)
+    matrix = dot(masked, wo[...].reshape(512, 1024), 1, 1).astype(jnp.bfloat16)
+    for head in range(heads):
+        gs[z, head] = matrix[:, head * HEAD : (head + 1) * HEAD]
+    weight_chunk(6)
     chain_recv(0, 2)
     chain_send(0, 3)
-    pass_weights(3)
-    finish_weights(2)
-    finish_weights(3)
-    for piece in range(4):
-        for step in (0, 2, 4):
+    chain_send(1, 1)
+    weight_chunk(7)
+    for step in range(1, count):
+        cot_copy(step).start()
+    finish_chunk(6)
+    finish_chunk(7)
+    for piece in range(1, 4):
+        for step in (0, 5, 6):
             weight_recv(piece, step)
-    chain_recv(1, 1)
-    chain_send(1, 2)
-    chain_recv(0, 3)
-
-    length = length_ref[0]
-
-    def project(block, carry):
+
+    def project(block):
         inputs = xs[block]
         start = pl.multiple_of(block * rows, rows)
         for pool, kept in ((wk, ks), (wv, vs), (wq, qs)):
             matrix = dot(inputs, pool[...].reshape(1024, 512), 1, 0).astype(jnp.bfloat16)
             for head in range(heads):
                 kept[head, pl.ds(start, rows), :] = matrix[:, head * HEAD : (head + 1) * HEAD]
-        return carry
-
-    lax.fori_loop(0, count, project, 0)
+
+    def project_hops(first, last):
+        def body(step, carry):
+            hop = step // 2
+            block = z + hop * (1 - 2 * lax.rem(step, 2))
+
+            @pl.when((block >= 0) & (block < count))
+            def _():
+                project(jnp.clip(block, 0, count - 1))
+
+            return carry
+
+        lax.fori_loop(first, last, body, 0)
+
+    project_hops(1, 6)
+    chain_recv(1, 1)
+    chain_send(1, 2)
+    chain_recv(0, 3)
+    project_hops(6, 8)
 
     def key_mask(amount):
         return lax.broadcasted_iota(jnp.int32, (amount, full), 1) < length
@@ -457,59 +514,40 @@
     row_at = z * rows + lax.broadcasted_iota(jnp.int32, attended.shape, 0)
     attended_ref[0] = jnp.where(row_at < length, attended, 0.0).astype(jnp.bfloat16)
 
-    chain_recv(1, 3)
-    for which in range(2):
-        for hop in range(1, count):
-            for side in range(2):
-                valid, copy = chain(which, side, hop)
-
-                @pl.when(valid)
-                def _():
-                    copy.wait_send()
-
-    def context_gradient(block, carry):
-        start = pl.multiple_of(block * rows, rows)
-        upstream = cs[block].astype(jnp.float32)
-        at = start + lax.broadcasted_iota(jnp.int32, upstream.shape, 0)
-        masked = jnp.where(at < length, upstream, 0.0).astype(jnp.bfloat16)
-        cs[block] = masked
-        matrix = dot(masked, wo[...].reshape(512, 1024), 1, 1).astype(jnp.bfloat16)
-        for head in range(heads):
-            piece = matrix[:, head * HEAD : (head + 1) * HEAD]
-            gs[head, pl.ds(start, rows), :] = piece
-            terms = piece.astype(jnp.float32) * ctx[head, pl.ds(start, rows), :].astype(jnp.float32)
-            deltas[head, pl.ds(start, rows), :] = jnp.sum(terms, axis=1, keepdims=True)
-        return carry
-
-    lax.fori_loop(0, count, context_gradient, 0)
-
-    columns = pl.ds(pl.multiple_of(z * width, width), width)
-    masked_slice = cs[:, :, columns].reshape(full, width)
+    for step in range(1, count):
+        source = lax.rem(z + count - step, count)
+        remote(cs.at[source], cs.at[source], 52 + step, (rep, dp, z)).wait_recv()
+    masked_slice = cs[...].reshape(full, width)
     for head in range(heads):
         part[head] = dot(ctx[head], masked_slice, 0, 0).astype(jnp.bfloat16)
 
     def part_copy(step):
         peer = lax.rem(group + step, 8)
         peer_dp = lax.rem(peer, 4)
-        return remote(part.at[peer_dp], part_in.at[step], 32 + step, (peer // 4, peer_dp, z))
+        return remote(part.at[peer_dp], part_in.at[step], 40 + step, (peer // 4, peer_dp, z))
 
     for step in range(1, 8):
         part_copy(step).start()
 
+    chain_recv(1, 3)
+
     def backward(head, carry):
-        queries, keys, values, grads = qs[head], ks[head], vs[head], gs[head]
+        queries, keys, values = qs[head], ks[head], vs[head]
+        grads = gs[:, head].reshape(full, HEAD)
+        terms = grads.astype(jnp.float32) * ctx[head].astype(jnp.float32)
+        deltas[...] = jnp.sum(terms, axis=1, keepdims=True)
         own_keys, own_values = ks[head, own, :], vs[head, own, :]
         scores = dot(queries, own_keys, 1, 1) * scale
         at = z * rows + lax.broadcasted_iota(jnp.int32, scores.shape, 1)
         attention = jnp.where(at < length, jnp.exp(scores - logsum[head]), 0.0)
         dv[head] = dot(attention.astype(jnp.bfloat16), grads, 0, 0).astype(jnp.bfloat16)
         grad_prob = dot(grads, own_values, 1, 1)
-        grad_score = (attention * (grad_prob - deltas[head])).astype(jnp.bfloat16)
+        grad_score = (attention * (grad_prob - deltas[...])).astype(jnp.bfloat16)
         dk[head] = (dot(grad_score, queries, 0, 0) * scale).astype(jnp.bfloat16)
         scores = dot(qs[head, own, :], keys, 1, 1) * scale
         attention = jnp.where(key_mask(rows), jnp.exp(scores - logsum[head, own, :]), 0.0)
-        grad_prob = dot(gs[head, own, :], values, 1, 1)
-        grad_score = (attention * (grad_prob - deltas[head, own, :])).astype(jnp.bfloat16)
+        grad_prob = dot(gs[z, head], values, 1, 1)
+        grad_score = (attention * (grad_prob - deltas[own, :])).astype(jnp.bfloat16)
         dq[head] = (dot(grad_score, keys, 1, 0) * scale).astype(jnp.bfloat16)
         return carry
 
@@ -523,7 +561,7 @@
 
     def slice_copy(step):
         return remote(
-            slices.at[z], slices.at[z], 40 + step, (rep, dp, lax.rem(z + step, count))
+            slices.at[z], slices.at[z], 48 + step, (rep, dp, lax.rem(z + step, count))
         )
 
     for step in range(1, count):
@@ -541,13 +579,24 @@
         grad_frames_ref[0, :, shard * 256 : (shard + 1) * 256] = added.astype(jnp.bfloat16)
 
     for piece in range(4):
-        for step in range(5):
+        for step in range(7):
             weight_copy(piece, step).wait_send()
+    for which in range(2):
+        for hop in range(1, count):
+            for side in range(2):
+                valid, copy = chain(which, side, hop)
+
+                @pl.when(valid)
+                def _():
+                    copy.wait_send()
+
+    for step in range(1, count):
+        cot_copy(step).wait_send()
     for step in range(1, 8):
         part_copy(step).wait_send()
     for step in range(1, count):
         source = lax.rem(z + count - step, count)
-        remote(slices.at[source], slices.at[source], 40 + step, (rep, dp, z)).wait_recv()
+        remote(slices.at[source], slices.at[source], 48 + step, (rep, dp, z)).wait_recv()
     for step in range(1, count):
         slice_copy(step).wait_send()
     for at in range(count):
@@ -556,6 +605,7 @@
 
 def fused(frames, lengths, cotangent, w_query, w_key, w_value, w_out):
     vmem = pl.BlockSpec(memory_space=pltpu.VMEM)
+    hbm = pl.BlockSpec(memory_space=pltpu.HBM)
     bf16, f32 = jnp.bfloat16, jnp.float32
     per_head = pltpu.VMEM((4, 512, HEAD), bf16)
     own_head = pltpu.VMEM((4, 128, HEAD), bf16)
@@ -566,11 +616,13 @@
             jax.ShapeDtypeStruct(frames.shape, bf16),
             jax.ShapeDtypeStruct(w_out.shape, f32),
         ),
-        in_specs=[vmem, pl.BlockSpec(memory_space=pltpu.SMEM)] + [vmem] * 5,
+        in_specs=[hbm, pl.BlockSpec(memory_space=pltpu.SMEM)] + [hbm] * 5,
         out_specs=(vmem, vmem, vmem),
         scratch_shapes=[
             pltpu.VMEM((4, 128, 1024), bf16),
-            pltpu.VMEM((4, 128, 1024), bf16),
+            pltpu.VMEM((128, 1024), bf16),
+            pltpu.VMEM((4, 128, 256), bf16),
+            pltpu.VMEM((4, 128, 256), bf16),
             pltpu.VMEM((4, 256, 512), bf16),
             pltpu.VMEM((4, 256, 512), bf16),
             pltpu.VMEM((4, 256, 512), bf16),
@@ -578,18 +630,19 @@
             per_head,
             per_head,
             per_head,
-            per_head,
+            pltpu.VMEM((4, 4, 128, HEAD), bf16),
             per_head,
             pltpu.VMEM((4, 512, 1), f32),
-            pltpu.VMEM((4, 512, 1), f32),
+            pltpu.VMEM((512, 1), f32),
             own_head,
             own_head,
             own_head,
             pltpu.VMEM((4, 128, 256), bf16),
             pltpu.VMEM((8, 128, 256), bf16),
             pltpu.VMEM((4, 128, 256), bf16),
-            pltpu.SemaphoreType.DMA((44,)),
-            pltpu.SemaphoreType.DMA((44,)),
+            pltpu.SemaphoreType.DMA((56,)),
+            pltpu.SemaphoreType.DMA((56,)),
+            pltpu.SemaphoreType.DMA((6,)),
         ],
         compiler_params=pltpu.CompilerParams(
             collective_id=0, has_side_effects=True, vmem_limit_bytes=48 * 1024 * 1024

time: 65.9 us -> 59.2 us (0.90)
  Pallas kernels: 56.4 us -> 49.1 us
    pallas_call x1, Pallas kernels: 56.4 us -> 49.1 us  [fused(): pl.pallas_call(fused_kernel, out_shape=(jax.ShapeDtypeStruct(frames.shape...]
where the time goes in v2:
time: 59.2 us; the launch traced here: 58.3 us
  Pallas kernels  49.1 us (83%)
  local copies, waits for them, and re-layouts  7.89 us (13%)
  between operations  1.3 us (2%)
    pallas_call x1, Pallas kernels, fused(): pl.pallas_call(fused_kernel, out_shape=(jax.ShapeDtypeStruct(frames.shape...  49.1 us
    unnamed x15, local copies, waits for them, and re-layouts  7.89 us

profile of v2, /device:TPU:13, one launch (start us, length us, event | category | flops | bytes accessed | tf_op | source)
XLA Modules:
  0.0 58.3 jit_solution(6321222786806093809)
XLA Ops:
  1.3 0.0 copy-start
  1.3 0.9 %copy-done = bf16[1,128,1024]{2,1,0:T(8,128)(2,1)S(1)} copy-done((bf16[1,128,1024]{2,1,0:T(8,128)(2,1)S(1)}, bf16[1,128,1024]{2,1,0:T(8,128)(2,1)}, u32[]{:S(2)}) %copy-start) | copy-done | bytes 262168
  2.2 0.0 copy-start.1
  2.2 0.9 %copy-done.1 = bf16[1,128,1024]{2,1,0:T(8,128)(2,1)S(1)} copy-done((bf16[1,128,1024]{2,1,0:T(8,128)(2,1)S(1)}, bf16[1,128,1024]{2,1,0:T(8,128)(2,1)}, u32[]{:S(2)}) %copy-start.1) | copy-done | bytes 262168
  3.2 0.0 copy-start.2
  3.2 0.9 %copy-done.2 = bf16[256,512]{1,0:T(8,128)(2,1)S(1)} copy-done((bf16[256,512]{1,0:T(8,128)(2,1)S(1)}, bf16[256,512]{1,0:T(8,128)(2,1)}, u32[]{:S(2)}) %copy-start.2) | copy-done | bytes 262168
  4.1 0.0 copy-start.3
  4.1 0.9 %copy-done.3 = bf16[256,512]{1,0:T(8,128)(2,1)S(1)} copy-done((bf16[256,512]{1,0:T(8,128)(2,1)S(1)}, bf16[256,512]{1,0:T(8,128)(2,1)}, u32[]{:S(2)}) %copy-start.3) | copy-done | bytes 262168
  5.1 0.0 copy-start.4
  5.1 0.9 %copy-done.4 = bf16[256,512]{1,0:T(8,128)(2,1)S(1)} copy-done((bf16[256,512]{1,0:T(8,128)(2,1)S(1)}, bf16[256,512]{1,0:T(8,128)(2,1)}, u32[]{:S(2)}) %copy-start.4) | copy-done | bytes 262168
  6.0 0.0 copy-start.5
  6.0 0.9 %copy-done.5 = bf16[128,1024]{1,0:T(8,128)(2,1)S(1)} copy-done((bf16[128,1024]{1,0:T(8,128)(2,1)S(1)}, bf16[128,1024]{1,0:T(8,128)(2,1)}, u32[]{:S(2)}) %copy-start.5) | copy-done | bytes 262168
  7.0 49.1 %shard_map.94 = (bf16[1,128,1024]{2,1,0:T(8,128)(2,1)S(1)}, bf16[1,128,1024]{2,1,0:T(8,128)(2,1)S(1)}, f32[128,1024]{1,0:T(8,128)S(1)}) custom-call(bf16[1,128,1024]{2,1,0:T(8,128)(2,1)S(1)} %copy-done, s32[1]{0:T(128)S(6)} %copy.13.length_ref, bf16[1,128,1024]{2,1,0:T(8,128)(2,1)S(1)} %copy-done.1, bf16[256,512]{1,0:T(8,128)(2,1)S(1)} %copy-done.2, ...), custom_call_target="tpu_custom_call" | custom-call | tf_op jit(solution)/shard_map/pallas_call | solution.py:612
  56.1 0.7 %copy.14 = bf16[1,128,1024]{2,1,0:T(8,128)(2,1)} copy(bf16[1,128,1024]{2,1,0:T(8,128)(2,1)S(1)} %get-tuple-element.6) | data formatting | bytes 524288
  56.8 0.7 %copy.15 = bf16[1,128,1024]{2,1,0:T(8,128)(2,1)} copy(bf16[1,128,1024]{2,1,0:T(8,128)(2,1)S(1)} %get-tuple-element.7) | data formatting | bytes 524288
  57.5 0.8 %copy.16 = f32[128,1024]{1,0:T(8,128)} copy(f32[128,1024]{1,0:T(8,128)S(1)} %get-tuple-element.8) | data formatting | bytes 1048576
Async XLA Ops:
  1.3 1.0 %copy-start = (bf16[1,128,1024]{2,1,0:T(8,128)(2,1)S(1)}, bf16[1,128,1024]{2,1,0:T(8,128)(2,1)}, u32[]{:S(2)}) copy-start(bf16[1,128,1024]{2,1,0:T(8,128)(2,1)} %frames_ref.1) | copy-start | bytes 786436
  2.2 0.9 %copy-start.1 = (bf16[1,128,1024]{2,1,0:T(8,128)(2,1)S(1)}, bf16[1,128,1024]{2,1,0:T(8,128)(2,1)}, u32[]{:S(2)}) copy-start(bf16[1,128,1024]{2,1,0:T(8,128)(2,1)} %cot_ref.1) | copy-start | bytes 786436
  3.2 0.9 %copy-start.2 = (bf16[256,512]{1,0:T(8,128)(2,1)S(1)}, bf16[256,512]{1,0:T(8,128)(2,1)}, u32[]{:S(2)}) copy-start(bf16[256,512]{1,0:T(8,128)(2,1)} %wq_ref.1) | copy-start | bytes 786436
  4.1 0.9 %copy-start.3 = (bf16[256,512]{1,0:T(8,128)(2,1)S(1)}, bf16[256,512]{1,0:T(8,128)(2,1)}, u32[]{:S(2)}) copy-start(bf16[256,512]{1,0:T(8,128)(2,1)} %wk_ref.1) | copy-start | bytes 786436
  5.1 0.9 %copy-start.4 = (bf16[256,512]{1,0:T(8,128)(2,1)S(1)}, bf16[256,512]{1,0:T(8,128)(2,1)}, u32[]{:S(2)}) copy-start(bf16[256,512]{1,0:T(8,128)(2,1)} %wv_ref.1) | copy-start | bytes 786436
  6.0 0.9 %copy-start.5 = (bf16[128,1024]{1,0:T(8,128)(2,1)S(1)}, bf16[128,1024]{1,0:T(8,128)(2,1)}, u32[]{:S(2)}) copy-start(bf16[128,1024]{1,0:T(8,128)(2,1)} %wo_ref.1) | copy-start | bytes 786436

commit v3 on v2

--- a/solution.py
+++ b/solution.py
@@ -448,10 +448,10 @@
     weight_chunk(6)
     chain_recv(0, 2)
     chain_send(0, 3)
+    for step in range(1, count):
+        cot_copy(step).start()
     chain_send(1, 1)
     weight_chunk(7)
-    for step in range(1, count):
-        cot_copy(step).start()
     finish_chunk(6)
     finish_chunk(7)
     for piece in range(1, 4):
@@ -480,8 +480,6 @@
         lax.fori_loop(first, last, body, 0)
 
     project_hops(1, 6)
-    chain_recv(1, 1)
-    chain_send(1, 2)
     chain_recv(0, 3)
     project_hops(6, 8)
 
@@ -504,16 +502,11 @@
         return carry
 
     lax.fori_loop(0, 4, forward, 0)
-    chain_recv(1, 2)
-    chain_send(1, 3)
+    chain_recv(1, 1)
+    chain_send(1, 2)
     lax.fori_loop(4, 8, forward, 0)
 
     own = pl.ds(pl.multiple_of(z * rows, rows), rows)
-    own_context = jnp.concatenate([ctx[head, own, :] for head in range(heads)], axis=1)
-    attended = dot(own_context, wo[...].reshape(512, 1024), 1, 0)
-    row_at = z * rows + lax.broadcasted_iota(jnp.int32, attended.shape, 0)
-    attended_ref[0] = jnp.where(row_at < length, attended, 0.0).astype(jnp.bfloat16)
-
     for step in range(1, count):
         source = lax.rem(z + count - step, count)
         remote(cs.at[source], cs.at[source], 52 + step, (rep, dp, z)).wait_recv()
@@ -528,6 +521,27 @@
 
     for step in range(1, 8):
         part_copy(step).start()
+    chain_recv(1, 2)
+    chain_send(1, 3)
+
+    own_context = jnp.concatenate([ctx[head, own, :] for head in range(heads)], axis=1)
+    attended = dot(own_context, wo[...].reshape(512, 1024), 1, 0)
+    row_at = z * rows + lax.broadcasted_iota(jnp.int32, attended.shape, 0)
+    attended_ref[0] = jnp.where(row_at < length, attended, 0.0).astype(jnp.bfloat16)
+
+    total = part[dp].astype(jnp.float32)
+    for step in range(1, 8):
+        part_copy(step).wait_recv()
+        total = total + part_in[step].astype(jnp.float32)
+    slices[z] = total.astype(jnp.bfloat16)
+
+    def slice_copy(step):
+        return remote(
+            slices.at[z], slices.at[z], 48 + step, (rep, dp, lax.rem(z + step, count))
+        )
+
+    for step in range(1, count):
+        slice_copy(step).start()
 
     chain_recv(1, 3)
 
@@ -552,20 +566,6 @@
         return carry
 
     lax.fori_loop(0, heads, backward, 0)
-
-    total = part[dp].astype(jnp.float32)
-    for step in range(1, 8):
-        part_copy(step).wait_recv()
-        total = total + part_in[step].astype(jnp.float32)
-    slices[z] = total.astype(jnp.bfloat16)
-
-    def slice_copy(step):
-        return remote(
-            slices.at[z], slices.at[z], 48 + step, (rep, dp, lax.rem(z + step, count))
-        )
-
-    for step in range(1, count):
-        slice_copy(step).start()
 
     grads = [
         jnp.concatenate([kept[head] for head in range(heads)], axis=1) for kept in (dq, dk, dv)

time: 59.2 us -> 56.7 us (0.958)
  Pallas kernels: 49.1 us -> 46.4 us
    pallas_call x1, Pallas kernels: 49.1 us -> 46.4 us  [fused(): pl.pallas_call(fused_kernel, out_shape=(jax.ShapeDtypeStruct(frames.shape...]
where the time goes in v3:
time: 56.7 us; the launch traced here: 55.6 us
  Pallas kernels  46.4 us (82%)
  local copies, waits for them, and re-layouts  7.89 us (14%)
  between operations  1.3 us (2%)
    pallas_call x1, Pallas kernels, fused(): pl.pallas_call(fused_kernel, out_shape=(jax.ShapeDtypeStruct(frames.shape...  46.4 us
    unnamed x15, local copies, waits for them, and re-layouts  7.89 us

profile of v3, /device:TPU:13, one launch (start us, length us, event | category | flops | bytes accessed | tf_op | source)
XLA Modules:
  0.0 55.6 jit_solution(14925288354657235818)
XLA Ops:
  1.3 0.0 copy-start
  1.3 0.9 %copy-done = bf16[1,128,1024]{2,1,0:T(8,128)(2,1)S(1)} copy-done((bf16[1,128,1024]{2,1,0:T(8,128)(2,1)S(1)}, bf16[1,128,1024]{2,1,0:T(8,128)(2,1)}, u32[]{:S(2)}) %copy-start) | copy-done | bytes 262168
  2.2 0.0 copy-start.1
  2.2 0.9 %copy-done.1 = bf16[1,128,1024]{2,1,0:T(8,128)(2,1)S(1)} copy-done((bf16[1,128,1024]{2,1,0:T(8,128)(2,1)S(1)}, bf16[1,128,1024]{2,1,0:T(8,128)(2,1)}, u32[]{:S(2)}) %copy-start.1) | copy-done | bytes 262168
  3.2 0.0 copy-start.2
  3.2 0.9 %copy-done.2 = bf16[256,512]{1,0:T(8,128)(2,1)S(1)} copy-done((bf16[256,512]{1,0:T(8,128)(2,1)S(1)}, bf16[256,512]{1,0:T(8,128)(2,1)}, u32[]{:S(2)}) %copy-start.2) | copy-done | bytes 262168
  4.1 0.0 copy-start.3
  4.1 0.9 %copy-done.3 = bf16[256,512]{1,0:T(8,128)(2,1)S(1)} copy-done((bf16[256,512]{1,0:T(8,128)(2,1)S(1)}, bf16[256,512]{1,0:T(8,128)(2,1)}, u32[]{:S(2)}) %copy-start.3) | copy-done | bytes 262168
  5.1 0.0 copy-start.4
  5.1 0.9 %copy-done.4 = bf16[256,512]{1,0:T(8,128)(2,1)S(1)} copy-done((bf16[256,512]{1,0:T(8,128)(2,1)S(1)}, bf16[256,512]{1,0:T(8,128)(2,1)}, u32[]{:S(2)}) %copy-start.4) | copy-done | bytes 262168
  6.0 0.0 copy-start.5
  6.0 0.9 %copy-done.5 = bf16[128,1024]{1,0:T(8,128)(2,1)S(1)} copy-done((bf16[128,1024]{1,0:T(8,128)(2,1)S(1)}, bf16[128,1024]{1,0:T(8,128)(2,1)}, u32[]{:S(2)}) %copy-start.5) | copy-done | bytes 262168
  7.0 46.4 %shard_map.94 = (bf16[1,128,1024]{2,1,0:T(8,128)(2,1)S(1)}, bf16[1,128,1024]{2,1,0:T(8,128)(2,1)S(1)}, f32[128,1024]{1,0:T(8,128)S(1)}) custom-call(bf16[1,128,1024]{2,1,0:T(8,128)(2,1)S(1)} %copy-done, s32[1]{0:T(128)S(6)} %copy.13.length_ref, bf16[1,128,1024]{2,1,0:T(8,128)(2,1)S(1)} %copy-done.1, bf16[256,512]{1,0:T(8,128)(2,1)S(1)} %copy-done.2, ...), custom_call_target="tpu_custom_call" | custom-call | tf_op jit(solution)/shard_map/pallas_call | solution.py:612
  53.4 0.7 %copy.14 = bf16[1,128,1024]{2,1,0:T(8,128)(2,1)} copy(bf16[1,128,1024]{2,1,0:T(8,128)(2,1)S(1)} %get-tuple-element.6) | data formatting | bytes 524288
  54.1 0.7 %copy.15 = bf16[1,128,1024]{2,1,0:T(8,128)(2,1)} copy(bf16[1,128,1024]{2,1,0:T(8,128)(2,1)S(1)} %get-tuple-element.7) | data formatting | bytes 524288
  54.8 0.8 %copy.16 = f32[128,1024]{1,0:T(8,128)} copy(f32[128,1024]{1,0:T(8,128)S(1)} %get-tuple-element.8) | data formatting | bytes 1048576
Async XLA Ops:
  1.3 1.0 %copy-start = (bf16[1,128,1024]{2,1,0:T(8,128)(2,1)S(1)}, bf16[1,128,1024]{2,1,0:T(8,128)(2,1)}, u32[]{:S(2)}) copy-start(bf16[1,128,1024]{2,1,0:T(8,128)(2,1)} %frames_ref.1) | copy-start | bytes 786436
  2.2 0.9 %copy-start.1 = (bf16[1,128,1024]{2,1,0:T(8,128)(2,1)S(1)}, bf16[1,128,1024]{2,1,0:T(8,128)(2,1)}, u32[]{:S(2)}) copy-start(bf16[1,128,1024]{2,1,0:T(8,128)(2,1)} %cot_ref.1) | copy-start | bytes 786436
  3.2 0.9 %copy-start.2 = (bf16[256,512]{1,0:T(8,128)(2,1)S(1)}, bf16[256,512]{1,0:T(8,128)(2,1)}, u32[]{:S(2)}) copy-start(bf16[256,512]{1,0:T(8,128)(2,1)} %wq_ref.1) | copy-start | bytes 786436
  4.1 0.9 %copy-start.3 = (bf16[256,512]{1,0:T(8,128)(2,1)S(1)}, bf16[256,512]{1,0:T(8,128)(2,1)}, u32[]{:S(2)}) copy-start(bf16[256,512]{1,0:T(8,128)(2,1)} %wk_ref.1) | copy-start | bytes 786436
  5.1 0.9 %copy-start.4 = (bf16[256,512]{1,0:T(8,128)(2,1)S(1)}, bf16[256,512]{1,0:T(8,128)(2,1)}, u32[]{:S(2)}) copy-start(bf16[256,512]{1,0:T(8,128)(2,1)} %wv_ref.1) | copy-start | bytes 786436
  6.0 0.9 %copy-start.5 = (bf16[128,1024]{1,0:T(8,128)(2,1)S(1)}, bf16[128,1024]{1,0:T(8,128)(2,1)}, u32[]{:S(2)}) copy-start(bf16[128,1024]{1,0:T(8,128)(2,1)} %wo_ref.1) | copy-start | bytes 786436

commit v4 on v3

--- a/solution.py
+++ b/solution.py
@@ -494,10 +494,10 @@
         scores = dot(qs[head, pl.ds(start, amount), :], ks[head], 1, 1) * scale
         scores = jnp.where(usable, scores, MASKED_SCORE)
         maxima = jnp.max(scores, axis=1, keepdims=True)
-        exponent = jnp.where(usable, jnp.exp(scores - maxima), 0.0)
+        exponent = jnp.exp(scores - maxima)
         totals = jnp.sum(exponent, axis=1, keepdims=True)
         mixed = dot(exponent.astype(jnp.bfloat16), vs[head], 1, 0)
-        ctx[head, pl.ds(start, amount), :] = (mixed / totals).astype(jnp.bfloat16)
+        ctx[head, pl.ds(start, amount), :] = (mixed * (1.0 / totals)).astype(jnp.bfloat16)
         logsum[head, pl.ds(start, amount), :] = maxima + jnp.log(totals)
         return carry
 

time: 56.7 us -> 56.6 us (level)
  no operation moved by 1% of the time
where the time goes in v4:
time: 56.6 us; the launch traced here: 55.5 us
  Pallas kernels  46.3 us (82%)
  local copies, waits for them, and re-layouts  7.89 us (14%)
  between operations  1.3 us (2%)
    pallas_call x1, Pallas kernels, fused(): pl.pallas_call(fused_kernel, out_shape=(jax.ShapeDtypeStruct(frames.shape...  46.3 us
    unnamed x15, local copies, waits for them, and re-layouts  7.89 us

profile of v4, /device:TPU:13, one launch (start us, length us, event | category | flops | bytes accessed | tf_op | source)
XLA Modules:
  0.0 55.5 jit_solution(9465885220809049777)
XLA Ops:
  1.3 0.0 copy-start
  1.3 0.9 %copy-done = bf16[1,128,1024]{2,1,0:T(8,128)(2,1)S(1)} copy-done((bf16[1,128,1024]{2,1,0:T(8,128)(2,1)S(1)}, bf16[1,128,1024]{2,1,0:T(8,128)(2,1)}, u32[]{:S(2)}) %copy-start) | copy-done | bytes 262168
  2.2 0.0 copy-start.1
  2.2 0.9 %copy-done.1 = bf16[1,128,1024]{2,1,0:T(8,128)(2,1)S(1)} copy-done((bf16[1,128,1024]{2,1,0:T(8,128)(2,1)S(1)}, bf16[1,128,1024]{2,1,0:T(8,128)(2,1)}, u32[]{:S(2)}) %copy-start.1) | copy-done | bytes 262168
  3.2 0.0 copy-start.2
  3.2 0.9 %copy-done.2 = bf16[256,512]{1,0:T(8,128)(2,1)S(1)} copy-done((bf16[256,512]{1,0:T(8,128)(2,1)S(1)}, bf16[256,512]{1,0:T(8,128)(2,1)}, u32[]{:S(2)}) %copy-start.2) | copy-done | bytes 262168
  4.1 0.0 copy-start.3
  4.1 0.9 %copy-done.3 = bf16[256,512]{1,0:T(8,128)(2,1)S(1)} copy-done((bf16[256,512]{1,0:T(8,128)(2,1)S(1)}, bf16[256,512]{1,0:T(8,128)(2,1)}, u32[]{:S(2)}) %copy-start.3) | copy-done | bytes 262168
  5.1 0.0 copy-start.4
  5.1 0.9 %copy-done.4 = bf16[256,512]{1,0:T(8,128)(2,1)S(1)} copy-done((bf16[256,512]{1,0:T(8,128)(2,1)S(1)}, bf16[256,512]{1,0:T(8,128)(2,1)}, u32[]{:S(2)}) %copy-start.4) | copy-done | bytes 262168
  6.0 0.0 copy-start.5
  6.0 0.9 %copy-done.5 = bf16[128,1024]{1,0:T(8,128)(2,1)S(1)} copy-done((bf16[128,1024]{1,0:T(8,128)(2,1)S(1)}, bf16[128,1024]{1,0:T(8,128)(2,1)}, u32[]{:S(2)}) %copy-start.5) | copy-done | bytes 262168
  7.0 46.3 %shard_map.94 = (bf16[1,128,1024]{2,1,0:T(8,128)(2,1)S(1)}, bf16[1,128,1024]{2,1,0:T(8,128)(2,1)S(1)}, f32[128,1024]{1,0:T(8,128)S(1)}) custom-call(bf16[1,128,1024]{2,1,0:T(8,128)(2,1)S(1)} %copy-done, s32[1]{0:T(128)S(6)} %copy.13.length_ref, bf16[1,128,1024]{2,1,0:T(8,128)(2,1)S(1)} %copy-done.1, bf16[256,512]{1,0:T(8,128)(2,1)S(1)} %copy-done.2, ...), custom_call_target="tpu_custom_call" | custom-call | tf_op jit(solution)/shard_map/pallas_call | solution.py:612
  53.3 0.7 %copy.14 = bf16[1,128,1024]{2,1,0:T(8,128)(2,1)} copy(bf16[1,128,1024]{2,1,0:T(8,128)(2,1)S(1)} %get-tuple-element.6) | data formatting | bytes 524288
  54.0 0.7 %copy.15 = bf16[1,128,1024]{2,1,0:T(8,128)(2,1)} copy(bf16[1,128,1024]{2,1,0:T(8,128)(2,1)S(1)} %get-tuple-element.7) | data formatting | bytes 524288
  54.7 0.8 %copy.16 = f32[128,1024]{1,0:T(8,128)} copy(f32[128,1024]{1,0:T(8,128)S(1)} %get-tuple-element.8) | data formatting | bytes 1048576
Async XLA Ops:
  1.3 1.0 %copy-start = (bf16[1,128,1024]{2,1,0:T(8,128)(2,1)S(1)}, bf16[1,128,1024]{2,1,0:T(8,128)(2,1)}, u32[]{:S(2)}) copy-start(bf16[1,128,1024]{2,1,0:T(8,128)(2,1)} %frames_ref.1) | copy-start | bytes 786436
  2.2 0.9 %copy-start.1 = (bf16[1,128,1024]{2,1,0:T(8,128)(2,1)S(1)}, bf16[1,128,1024]{2,1,0:T(8,128)(2,1)}, u32[]{:S(2)}) copy-start(bf16[1,128,1024]{2,1,0:T(8,128)(2,1)} %cot_ref.1) | copy-start | bytes 786436
  3.2 0.9 %copy-start.2 = (bf16[256,512]{1,0:T(8,128)(2,1)S(1)}, bf16[256,512]{1,0:T(8,128)(2,1)}, u32[]{:S(2)}) copy-start(bf16[256,512]{1,0:T(8,128)(2,1)} %wq_ref.1) | copy-start | bytes 786436
  4.1 0.9 %copy-start.3 = (bf16[256,512]{1,0:T(8,128)(2,1)S(1)}, bf16[256,512]{1,0:T(8,128)(2,1)}, u32[]{:S(2)}) copy-start(bf16[256,512]{1,0:T(8,128)(2,1)} %wk_ref.1) | copy-start | bytes 786436
  5.1 0.9 %copy-start.4 = (bf16[256,512]{1,0:T(8,128)(2,1)S(1)}, bf16[256,512]{1,0:T(8,128)(2,1)}, u32[]{:S(2)}) copy-start(bf16[256,512]{1,0:T(8,128)(2,1)} %wv_ref.1) | copy-start | bytes 786436
  6.0 0.9 %copy-start.5 = (bf16[128,1024]{1,0:T(8,128)(2,1)S(1)}, bf16[128,1024]{1,0:T(8,128)(2,1)}, u32[]{:S(2)}) copy-start(bf16[128,1024]{1,0:T(8,128)(2,1)} %wo_ref.1) | copy-start | bytes 786436
